TPU v7x, 256 devices: a whole 4x4x8 slice. The times are simulated.
256 devices in a mesh: dp: 128 (over y_hi, x, z, core), dup: 2 (over y_lo).
Axes of the slice: x: 4, y: 4 (y_hi: 2, y_lo: 2; y = y_hi * 2 + y_lo), z: 8, core: 2. Of those that a mesh axis runs over, the one named last changes fastest.
Arguments:
- visual_embedding_matrix: bfloat16 [131072, 1024], P(('dp', 'dup')), may hold values from -6 to 6
- description_matrix: bfloat16 [131072, 1024], P(('dp', 'dup')), may hold values from -6 to 6
- sharpness_factor: float32 [1], replicated, may hold values from 0.05 to 0.1
Outputs:
- image_loss: float32 [131072], P(('dp', 'dup'))
- text_loss: float32 [131072], P(('dp', 'dup'))
- image_grad: float32 [131072, 1024], P(('dp', 'dup'))
- text_grad: float32 [131072, 1024], P(('dp', 'dup'))
All inputs are finite; a program needn't handle non-finite values.
Results may differ from a plain program's by a relative error of at most 0.0014.
Values may be sent and summed in bfloat16 or wider, within the bound.
A program may use at most 128 MiB of HBM per device.

v0:
```python
import jax
import jax.numpy as jnp
from jax import lax
from jax.sharding import PartitionSpec as P

NEIGH = 2


def passed_along(value, axis, by):
    size = lax.axis_size(axis)
    return lax.ppermute(value, axis, [(i, (i + by) % size) for i in range(size)])


def combined_all(value, axis, combine):
    everything = jax.tree.map(lambda part: lax.all_gather(part, axis), value)
    leading = jax.tree.map(lambda part: part[0], everything)

    def step(k, so_far):
        return combine(so_far, jax.tree.map(lambda part: part[k], everything))

    return lax.fori_loop(1, lax.axis_size(axis), step, leading)


def pairwise_logits(left, right, similarity_multiplier):
    return (
        lax.dot_general(left, right, (((1,), (1,)), ((), ())), preferred_element_type=jnp.float32)
        * similarity_multiplier
    )


def left_product(softmax_weights, right):
    return lax.dot_general(
        softmax_weights, right, (((0,), (0,)), ((), ())), preferred_element_type=jnp.float32
    )


def merge_pair(first, second):
    top = jnp.maximum(first[0], second[0])
    return (top, first[1] * jnp.exp(first[0] - top) + second[1] * jnp.exp(second[0] - top))


def shards(visual_embedding_matrix, description_matrix, sharpness_factor):
    similarity_multiplier = sharpness_factor[0]
    half = visual_embedding_matrix.shape[0]
    start = lax.axis_index("dup") * half
    captions = lax.all_gather(description_matrix, "dup", axis=0, tiled=True)
    blocks = [captions]
    travelling_operand = captions
    for step in range(NEIGH):
        travelling_operand = passed_along(travelling_operand, "dp", -1)
        blocks.append(travelling_operand)
    tiles = [
        pairwise_logits(visual_embedding_matrix, block, similarity_multiplier) for block in blocks
    ]
    row_top = tiles[0].max(axis=1)
    for tile in tiles[1:]:
        row_top = jnp.maximum(row_top, tile.max(axis=1))
    row_total = jnp.zeros_like(row_top)
    for tile in tiles:
        row_total = row_total + jnp.exp(tile - row_top[:, None]).sum(axis=1)
    row_lse = row_top + jnp.log(row_total)
    matched_logits = jnp.diagonal(lax.dynamic_slice_in_dim(tiles[0], start, half, 1))
    image_loss = row_lse - matched_logits
    column_peak = jnp.stack([tile.max(axis=0) for tile in tiles])
    col_total = jnp.stack([jnp.exp(tile - tile.max(axis=0)[None, :]).sum(axis=0) for tile in tiles])
    column_peak, col_total = combined_all((column_peak, col_total), "dup", merge_pair)
    carried = (column_peak[NEIGH], col_total[NEIGH])
    for index in range(NEIGH - 1, -1, -1):
        carried = passed_along((carried[0], carried[1]), "dp", 1)
        carried = merge_pair(carried, (column_peak[index], col_total[index]))
    column_lse = carried[0] + jnp.log(carried[1])
    text_loss = lax.dynamic_slice_in_dim(column_lse, start, half, 0) - matched_logits
    lse_list = [column_lse]
    moving_lse = column_lse
    for step in range(NEIGH):
        moving_lse = passed_along(moving_lse, "dp", -1)
        lse_list.append(moving_lse)
    grad_rows = jnp.zeros((half, visual_embedding_matrix.shape[1]), jnp.float32)
    partials = []
    for index in range(NEIGH + 1):
        softmax_weights = (
            jnp.exp(tiles[index] - row_lse[:, None])
            + jnp.exp(tiles[index] - lse_list[index][None, :])
        ).astype(jnp.bfloat16)
        grad_rows = grad_rows + jnp.dot(
            softmax_weights, blocks[index], preferred_element_type=jnp.float32
        )
        partials.append(left_product(softmax_weights, visual_embedding_matrix))
    shares = lax.psum_scatter(jnp.stack(partials), "dup", scatter_dimension=1, tiled=True)
    caption_sum = shares[NEIGH]
    for index in range(NEIGH - 1, -1, -1):
        caption_sum = passed_along(caption_sum, "dp", 1) + shares[index]
    image_grad = (
        similarity_multiplier * grad_rows
        - 2.0 * similarity_multiplier * description_matrix.astype(jnp.float32)
    )
    text_grad = (
        similarity_multiplier * caption_sum
        - 2.0 * similarity_multiplier * visual_embedding_matrix.astype(jnp.float32)
    )
    return (image_loss, text_loss, image_grad, text_grad)


def solution(mesh):
    return jax.shard_map(
        shards,
        mesh=mesh,
        in_specs=(P(("dp", "dup"), None), P(("dp", "dup"), None), P()),
        out_specs=(
            P(("dp", "dup")),
            P(("dp", "dup")),
            P(("dp", "dup"), None),
            P(("dp", "dup"), None),
        ),
        check_vma=False,
    )
```

profile of v0, /device:TPU:16, one launch (start us, length us, event | category | flops | bytes accessed | tf_op | source)
XLA Modules:
  0.0 389.6 jit_solution(118348895222100621)
XLA Ops:
  7.2 0.0 all-gather.6.cloned.1.call-start
  7.2 0.7 all-gather.6.cloned.1.call-update
  7.9 0.0 reduce-scatter.2.cloned.1.call-start
  7.9 42.6 %all-gather.6.cloned.1.call-done = bf16[1024,1024]{1,0:T(8,128)(2,1)} async-done(((bf16[512,1024]{1,0:T(8,128)(2,1)}), bf16[1024,1024]{1,0:T(8,128)(2,1)}) %all-gather.6.cloned.1.call-update) | async-done | bytes 2097168 | tf_op jit(solution)/shard_map/all_gather | solution.py:46
  50.5 5.1 %collective-permute-start = (bf16[1024,1024]{1,0:T(8,128)(2,1)}, bf16[1024,1024]{1,0:T(8,128)(2,1)S(1)}, u32[]{:S(2)}, u32[]{:S(2)}) collective-permute-start(bf16[1024,1024]{1,0:T(8,128)(2,1)} %all-gather.6.cloned.1.call-done), channel_id=1, source_target_pairs={{0,254},{2,0},{4,2},{6,4},{8,6},{10,8},{12,10},{14,12},{16,14},{18... | collective-permute-start | bytes 6291464 | tf_op jit(solution)/shard_map/ppermute | solution.py:11
  55.7 23.9 %collective-permute-done = bf16[1024,1024]{1,0:T(8,128)(2,1)S(1)} collective-permute-done((bf16[1024,1024]{1,0:T(8,128)(2,1)}, bf16[1024,1024]{1,0:T(8,128)(2,1)S(1)}, u32[]{:S(2)}, u32[]{:S(2)}) %collective-permute-start) | collective-permute-done | bytes 2097184 | tf_op jit(solution)/shard_map/ppermute | solution.py:11
  79.5 7.5 %collective-permute-start.1 = (bf16[1024,1024]{1,0:T(8,128)(2,1)S(1)}, bf16[1024,1024]{1,0:T(8,128)(2,1)S(1)}, u32[]{:S(2)}, u32[]{:S(2)}) collective-permute-start(bf16[1024,1024]{1,0:T(8,128)(2,1)S(1)} %collective-permute-done), channel_id=1, source_target_pairs={{0,254},{2,0},{4,2},{6,4},{8,6},{10,8},{12,10},{14,12},{16,14},{18... | collective-permute-start | bytes 6291464 | tf_op jit(solution)/shard_map/ppermute | solution.py:11
  87.7 0.0 copy-start.7
  87.7 3.4 fusion.12
  91.1 1.4 fusion.13
  92.5 18.1 %collective-permute-done.1 = bf16[1024,1024]{1,0:T(8,128)(2,1)S(1)} collective-permute-done((bf16[1024,1024]{1,0:T(8,128)(2,1)S(1)}, bf16[1024,1024]{1,0:T(8,128)(2,1)S(1)}, u32[]{:S(2)}, u32[]{:S(2)}) %collective-permute-start.1) | collective-permute-done | bytes 2097184 | tf_op jit(solution)/shard_map/ppermute | solution.py:11
  110.6 1.4 fusion.14
  112.0 4.4 %all-gather.2 = f32[2,3,1024]{2,1,0:T(4,128)S(1)} all-gather(f32[1,3,1024]{2,1,0:T(4,128)S(1)} %maximum_bitcast_fusion), channel_id=2, replica_groups=mesh['dp'=128,'dup'=2] {'dup'}, dimensions={0}, use_global_device_ids=true | all-gather | bytes 36864 | tf_op jit(solution)/shard_map/all_gather | solution.py:15
  116.4 2.1 exponential_reduce_fusion.1
  118.5 4.4 %all-gather.3 = f32[2,3,1024]{2,1,0:T(4,128)S(1)} all-gather(f32[1,3,1024]{2,1,0:T(4,128)S(1)} %maximum_bitcast_fusion.1), channel_id=3, replica_groups=mesh['dp'=128,'dup'=2] {'dup'}, dimensions={0}, use_global_device_ids=true | all-gather | bytes 36864 | tf_op jit(solution)/shard_map/all_gather | solution.py:15
  123.0 0.1 collective-permute-start.2
  123.1 0.1 collective-permute-start.4
  123.2 8.6 %collective-permute-done.2 = f32[1024]{0:T(1024)S(1)} collective-permute-done((f32[1024]{0:T(1024)S(1)}, f32[1024]{0:T(1024)S(1)}, u32[]{:S(2)}, u32[]{:S(2)}) %collective-permute-start.2) | collective-permute-done | bytes 4128 | tf_op jit(solution)/shard_map/ppermute | solution.py:11
  131.8 0.1 collective-permute-done.4
  132.0 0.1 collective-permute-start.5
  132.0 0.1 collective-permute-start.3
  132.1 0.1 constant_dynamic-slice_fusion
  132.2 4.5 %gather_fusion = f32[512]{0:T(512)S(1)} fusion(f32[512,512]{1,0:T(8,128)S(1)} %constant_dynamic-slice_fusion, s32[512]{0:T(512)S(1)} %bitcast.82), kind=kCustom, calls=%fused_computation | custom fusion | bytes 8192 | tf_op jit(solution)/shard_map/jit(diagonal)/cond/branch_0_fun/gather | solution.py:62
  136.8 4.0 %collective-permute-done.5 = f32[1024]{0:T(1024)S(1)} collective-permute-done((f32[1024]{0:T(1024)S(1)}, f32[1024]{0:T(1024)S(1)}, u32[]{:S(2)}, u32[]{:S(2)}) %collective-permute-start.5) | collective-permute-done | bytes 4128 | tf_op jit(solution)/shard_map/ppermute | solution.py:11
  140.8 0.1 collective-permute-done.3
  140.9 3.6 collective-permute-start.6
  144.5 0.7 fusion.16
  145.1 2.8 convolution_bitcast_fusion.2
  148.0 5.3 %collective-permute-start.7 = (f32[1024]{0:T(1024)S(1)}, f32[1024]{0:T(1024)S(1)}, u32[]{:S(2)}, u32[]{:S(2)}) collective-permute-start(f32[1024]{0:T(1024)S(1)} %collective-permute-done.6), channel_id=1, source_target_pairs={{0,254},{2,0},{4,2},{6,4},{8,6},{10,8},{12,10},{14,12},{16,14},{18... | collective-permute-start | bytes 12296 | tf_op jit(solution)/shard_map/ppermute | solution.py:11
  153.3 1.4 convolution_bitcast_fusion.1
  154.7 0.0 collective-permute-done.7
  154.7 1.4 convolution_bitcast_fusion
  156.2 4.8 %pad_maximum_fusion = f32[3,1024,1024]{2,1,0:T(8,128)} fusion(f32[1,1024,1024]{2,1,0:T(8,128)S(1)} %convolution_bitcast_fusion, f32[1,1024,1024]{2,1,0:T(8,128)S(1)} %convolution_bitcast_fusion.1, f32[1,1024,1024]{2,1,0:T(8,128)S(1)} %convolution_bitcast_fusion.2), kind=kLoop, calls=%fused_computation.1 | loop fusion | flops 6291456 | bytes 25165824 | tf_op jit(solution)/shard_map/stack | solution.py:89
  161.0 0.0 reduce-scatter.2.cloned.1.call-update
  161.0 149.6 %reduce-scatter.2.cloned.1.call-done = f32[3,512,1024]{2,1,0:T(8,128)} async-done(((f32[3,1024,1024]{2,1,0:T(8,128)}), f32[3,512,1024]{2,1,0:T(8,128)}) %reduce-scatter.2.cloned.1.call-update) | async-done | bytes 6291472 | tf_op jit(solution)/shard_map/reduce_scatter | solution.py:89
  310.7 1.7 slice_bitcast_fusion.2
  312.4 0.1 collective-permute-start.8
  312.5 31.2 %collective-permute-done.8 = f32[512,1024]{1,0:T(8,128)S(1)} collective-permute-done((f32[512,1024]{1,0:T(8,128)S(1)}, f32[512,1024]{1,0:T(8,128)S(1)}, u32[]{:S(2)}, u32[]{:S(2)}) %collective-permute-start.8) | collective-permute-done | bytes 2097184 | tf_op jit(solution)/shard_map/ppermute | solution.py:11
  343.7 3.3 fusion.3
  346.9 3.2 fusion.10
  350.1 0.0 copy-start.6
  350.1 1.4 fusion.11
  351.6 0.1 copy-done.5
  351.7 0.3 copy-done.6
  352.0 0.7 copy-done.12
  352.7 3.0 multiply_subtract_fusion
  355.7 22.8 %collective-permute-done.9 = f32[512,1024]{1,0:T(8,128)} collective-permute-done((f32[512,1024]{1,0:T(8,128)}, f32[512,1024]{1,0:T(8,128)}, u32[]{:S(2)}, u32[]{:S(2)}) %collective-permute-start.9) | collective-permute-done | bytes 2097184 | tf_op jit(solution)/shard_map/ppermute | solution.py:11
  378.4 4.3 %fusion.2 = f32[512,1024]{1,0:T(8,128)} fusion(f32[512,1024]{1,0:T(8,128)} %collective-permute-done.9, f32[3,512,1024]{2,1,0:T(8,128)} %reduce-scatter.2.cloned.1.call-done, bf16[512,1024]{1,0:T(8,128)(2,1)S(1)} %copy-done.8, f32[]{:T(128)S(6)} %mul.71, f32[]{:T(128)} %bitcast.78), kind=kLoop, calls=%fused_computation.8 | loop fusion | flops 2621440 | bytes 7340040 | tf_op jit(solution)/shard_map/sub | solution.py:98
  (31 shorter events, 0.2 us)
Async XLA Ops:
  7.2 43.4 %all-gather.6.cloned.1.call-start = ((), (), s32[]{:S(2)}) async-start(), calls=%async_computation.1 | async-start | bytes 3145728 | tf_op jit(solution)/shard_map/all_gather | solution.py:46
  7.9 302.8 %reduce-scatter.2.cloned.1.call-start = ((), (), s32[]{:S(2)}) async-start(), calls=%async_computation.2 | async-start | bytes 18874368 | tf_op jit(solution)/shard_map/reduce_scatter | solution.py:89
  50.5 29.0 %collective-permute-start = (bf16[1024,1024]{1,0:T(8,128)(2,1)}, bf16[1024,1024]{1,0:T(8,128)(2,1)S(1)}, u32[]{:S(2)}, u32[]{:S(2)}) collective-permute-start(bf16[1024,1024]{1,0:T(8,128)(2,1)} %all-gather.6.cloned.1.call-done), channel_id=1, source_target_pairs={{0,254},{2,0},{4,2},{6,4},{8,6},{10,8},{12,10},{14,12},{16,14},{18... | collective-permute-start | bytes 6291464 | tf_op jit(solution)/shard_map/ppermute | solution.py:11
  79.5 11.6 %copy-start.9 = (bf16[1024,1024]{1,0:T(8,128)(2,1)}, bf16[1024,1024]{1,0:T(8,128)(2,1)S(1)}, u32[]{:S(2)}) copy-start(bf16[1024,1024]{1,0:T(8,128)(2,1)S(1)} %collective-permute-done) | copy-start | bytes 6291460
  79.5 31.1 %collective-permute-start.1 = (bf16[1024,1024]{1,0:T(8,128)(2,1)S(1)}, bf16[1024,1024]{1,0:T(8,128)(2,1)S(1)}, u32[]{:S(2)}, u32[]{:S(2)}) collective-permute-start(bf16[1024,1024]{1,0:T(8,128)(2,1)S(1)} %collective-permute-done), channel_id=1, source_target_pairs={{0,254},{2,0},{4,2},{6,4},{8,6},{10,8},{12,10},{14,12},{16,14},{18... | collective-permute-start | bytes 6291464 | tf_op jit(solution)/shard_map/ppermute | solution.py:11
  87.7 3.4 copy-start.7
  92.5 24.0 %copy-start = (f32[512,1024]{1,0:T(8,128)}, f32[512,1024]{1,0:T(8,128)S(1)}, u32[]{:S(2)}) copy-start(f32[512,1024]{1,0:T(8,128)S(1)} %get-tuple-element.53) | copy-start | bytes 6291460
  110.6 1.4 copy-start.11
  112.0 6.5 %copy-start.3 = (f32[512,1024]{1,0:T(8,128)}, f32[512,1024]{1,0:T(8,128)S(1)}, u32[]{:S(2)}) copy-start(f32[512,1024]{1,0:T(8,128)S(1)} %get-tuple-element.51) | copy-start | bytes 6291460
  123.0 8.8 %collective-permute-start.2 = (f32[1024]{0:T(1024)S(1)}, f32[1024]{0:T(1024)S(1)}, u32[]{:S(2)}, u32[]{:S(2)}) collective-permute-start(f32[1024]{0:T(1024)S(1)} %bitcast.94), channel_id=1, source_target_pairs={{0,2},{2,4},{4,6},{6,8},{8,10},{10,12},{12,14},{14,16},{16,18},{18... | collective-permute-start | bytes 12296 | tf_op jit(solution)/shard_map/ppermute | solution.py:11
  123.1 8.8 %collective-permute-start.4 = (f32[1024]{0:T(1024)S(1)}, f32[1024]{0:T(1024)S(1)}, u32[]{:S(2)}, u32[]{:S(2)}) collective-permute-start(f32[1024]{0:T(1024)S(1)} %bitcast.93), channel_id=1, source_target_pairs={{0,2},{2,4},{4,6},{6,8},{8,10},{10,12},{12,14},{14,16},{16,18},{18... | collective-permute-start | bytes 12296 | tf_op jit(solution)/shard_map/ppermute | solution.py:11
  132.0 8.8 %collective-permute-start.5 = (f32[1024]{0:T(1024)S(1)}, f32[1024]{0:T(1024)S(1)}, u32[]{:S(2)}, u32[]{:S(2)}) collective-permute-start(f32[1024]{0:T(1024)S(1)} %get-tuple-element.34), channel_id=1, source_target_pairs={{0,2},{2,4},{4,6},{6,8},{8,10},{10,12},{12,14},{14,16},{16,18},{18... | collective-permute-start | bytes 12296 | tf_op jit(solution)/shard_map/ppermute | solution.py:11
  132.0 8.8 %collective-permute-start.3 = (f32[1024]{0:T(1024)S(1)}, f32[1024]{0:T(1024)S(1)}, u32[]{:S(2)}, u32[]{:S(2)}) collective-permute-start(f32[1024]{0:T(1024)S(1)} %get-tuple-element.35), channel_id=1, source_target_pairs={{0,2},{2,4},{4,6},{6,8},{8,10},{10,12},{12,14},{14,16},{16,18},{18... | collective-permute-start | bytes 12296 | tf_op jit(solution)/shard_map/ppermute | solution.py:11
  140.9 7.1 %collective-permute-start.6 = (f32[1024]{0:T(1024)S(1)}, f32[1024]{0:T(1024)S(1)}, u32[]{:S(2)}, u32[]{:S(2)}) collective-permute-start(f32[1024]{0:T(1024)S(1)} %log_add_fusion), channel_id=1, source_target_pairs={{0,254},{2,0},{4,2},{6,4},{8,6},{10,8},{12,10},{14,12},{16,14},{18... | collective-permute-start | bytes 12296 | tf_op jit(solution)/shard_map/ppermute | solution.py:11
  145.1 8.1 %copy-start.1 = (f32[512,1024]{1,0:T(8,128)S(1)}, f32[512,1024]{1,0:T(8,128)}, u32[]{:S(2)}) copy-start(f32[512,1024]{1,0:T(8,128)} %copy-done) | copy-start | bytes 6291460
  145.1 8.1 %copy-start.8 = (bf16[512,1024]{1,0:T(8,128)(2,1)S(1)}, bf16[512,1024]{1,0:T(8,128)(2,1)}, u32[]{:S(2)}) copy-start(bf16[512,1024]{1,0:T(8,128)(2,1)} %param.3) | copy-start | bytes 3145732
  147.9 6.8 %copy-start.4 = (f32[512,1024]{1,0:T(8,128)S(1)}, f32[512,1024]{1,0:T(8,128)}, u32[]{:S(2)}) copy-start(f32[512,1024]{1,0:T(8,128)} %copy-done.3) | copy-start | bytes 6291460
  148.0 6.7 %collective-permute-start.7 = (f32[1024]{0:T(1024)S(1)}, f32[1024]{0:T(1024)S(1)}, u32[]{:S(2)}, u32[]{:S(2)}) collective-permute-start(f32[1024]{0:T(1024)S(1)} %collective-permute-done.6), channel_id=1, source_target_pairs={{0,254},{2,0},{4,2},{6,4},{8,6},{10,8},{12,10},{14,12},{16,14},{18... | collective-permute-start | bytes 12296 | tf_op jit(solution)/shard_map/ppermute | solution.py:11
  312.4 31.3 %collective-permute-start.8 = (f32[512,1024]{1,0:T(8,128)S(1)}, f32[512,1024]{1,0:T(8,128)S(1)}, u32[]{:S(2)}, u32[]{:S(2)}) collective-permute-start(f32[512,1024]{1,0:T(8,128)S(1)} %slice_bitcast_fusion.2), channel_id=1, source_target_pairs={{0,2},{2,4},{4,6},{6,8},{8,10},{10,12},{12,14},{14,16},{16,18},{18... | collective-permute-start | bytes 6291464 | tf_op jit(solution)/shard_map/ppermute | solution.py:11
  346.9 31.5 %collective-permute-start.9 = (f32[512,1024]{1,0:T(8,128)}, f32[512,1024]{1,0:T(8,128)}, u32[]{:S(2)}, u32[]{:S(2)}) collective-permute-start(f32[512,1024]{1,0:T(8,128)} %fusion.3), channel_id=1, source_target_pairs={{0,2},{2,4},{4,6},{6,8},{8,10},{10,12},{12,14},{14,16},{16,18},{18... | collective-permute-start | bytes 6291464 | tf_op jit(solution)/shard_map/ppermute | solution.py:11
  346.9 3.2 copy-start.2
  346.9 3.2 copy-start.10
  350.1 1.6 copy-start.5
  350.1 1.8 copy-start.6
  350.1 2.5 copy-start.12
Sparse Core Ops, SparseCore 0:
  9.8 40.6 all-gather.5
  161.2 149.4 reduce-scatter.1
where the time goes:
time: 390 us
  waiting for transfers between devices  302 us (77%)
  starting transfers between devices  22 us (6%)
  matrix products  19.4 us (5%)
  other arithmetic  15.2 us (4%)
  between operations  14.9 us (4%)
  blocking collectives  8.83 us (2%)
  local copies, waits for them, and re-layouts  7.46 us (2%)
    reduce_scatter x1, waiting for transfers between devices, shards(): lax.psum_scatter(jnp.stack(partials), 'dup', scatter_dimension=1, tiled=T...  150 us
    ppermute x10, waiting for transfers between devices, passed_along(): lax.ppermute(value, axis, [(i, (i + by) % size) for i in range(size)])  109 us
    all_gather x1, waiting for transfers between devices, shards(): captions = lax.all_gather(description_matrix, 'dup', axis=0, tiled=True)  42.6 us
    ppermute x10, starting transfers between devices, passed_along(): lax.ppermute(value, axis, [(i, (i + by) % size) for i in range(size)])  22 us
    all_gather x2, blocking collectives, combined_all(): everything = jax.tree.map(lambda part: lax.all_gather(part, axis), value)  8.83 us
  transfers between devices with their start and end apart: 12, of which 10 were waited for; matrix products, arithmetic and copies ran while one was open for 6% of the time, Pallas kernels for 0%

commit v1 on v0

v1 whole, which is shorter than its diff:
```python
import functools
import math

import jax
import jax.numpy as jnp
from jax import lax
from jax.experimental import pallas as pl
from jax.experimental.pallas import tpu as pltpu
from jax.sharding import PartitionSpec as P

MESH = pl.DeviceIdType.MESH
LOG2E = math.log2(math.e)
LN2 = math.log(2.0)
CHUNKS = 8
LOW = -1e30

FIRST_EVEN = [
    (0, 0, 0), (0, 0, 1), (1, 2, 0), (2, 2, 1), (4, 1, 0), (4, 4, 0),
    (5, 4, 1), (6, 3, 0), (7, 5, 0), (8, 1, 1), (8, 3, 1), (8, 5, 1),
]
FIRST_ODD = [
    (0, 0, 0), (0, 0, 1), (4, 1, 0), (4, 2, 0), (5, 4, 0), (5, 4, 1),
    (6, 5, 0), (7, 2, 1), (7, 3, 0), (8, 1, 1), (8, 5, 1), (8, 3, 1),
]
SECOND_EVEN = [
    (1, 0, 0), (1, 0, 1), (2, 1, 0), (2, 1, 1), (2, 2, 0), (2, 2, 1),
    (3, 3, 0), (3, 3, 1), (3, 4, 0), (4, 4, 1), (4, 5, 0), (4, 5, 1),
    (4, 6, 0), (5, 6, 1), (5, 8, 0), (5, 8, 1), (5, 10, 0), (6, 10, 1),
    (6, 7, 0), (6, 11, 0), (6, 9, 0), (8, 7, 1), (9, 11, 1), (9, 9, 1),
]
SECOND_ODD = [
    (1, 0, 0), (1, 0, 1), (2, 1, 0), (2, 1, 1), (2, 2, 0), (2, 2, 1),
    (3, 3, 0), (3, 3, 1), (3, 6, 0), (4, 6, 1), (4, 8, 0), (4, 8, 1),
    (4, 10, 0), (5, 10, 1), (5, 4, 0), (5, 4, 1), (5, 5, 0), (6, 7, 0),
    (6, 11, 0), (6, 9, 0), (8, 7, 1), (9, 11, 1), (9, 9, 1), (9, 5, 1),
]


def looked_up(index, odd, even_list, odd_list):
    def words(entries):
        codes = [k * 32 + slot * 2 + part for k, slot, part in entries]
        codes += [0] * (-len(codes) % 3)
        return [sum(c << (9 * i) for i, c in enumerate(codes[at : at + 3])) for at in range(0, len(codes), 3)]

    group = index // 3
    word = jnp.int32(0)
    for at, (even_word, odd_word) in enumerate(zip(words(even_list), words(odd_list))):
        word = jnp.where(group == at, jnp.where(odd == 1, odd_word, even_word), word)
    code = lax.shift_right_logical(word, 9 * (index - group * 3)) & 511
    return code // 32, (code % 32) // 2, code % 2


def wide(column, count):
    return jnp.concatenate([column] * (count // 128), axis=1)


def log2(value):
    return jnp.log(value) * LOG2E


def merged(first, second):
    top = jnp.maximum(first, second)
    return top + log2(jnp.exp2(first - top) + jnp.exp2(second - top))


def kernel(
    n_dp, group,
    scale_ref, v_hbm, t_hbm,
    image_loss, text_loss, image_grad, text_grad,
    rows_buf, scores, acc, peak, total, own_col, got_col, own_row, got_row, lanes, column, losses, diagonal,
    send_sem, recv_sem, col_send, col_recv, row_send, row_recv, lane_send, lane_recv, load_sem, out_sem,
):
    half, width = v_hbm.shape
    chunk = half // CHUNKS
    part_rows = half // 2
    per_part = CHUNKS // 2
    b = lax.axis_index("dp")
    h = lax.axis_index("dup")
    odd = b % 2
    place = b % group
    flip_t = jnp.where(place >= group - 2, 1, 0)
    flip_v = jnp.where(place < 2, 1, 0)

    def block(by):
        return (b + by + n_dp) % n_dp

    other = (b, 1 - h)
    mate = (b + 1 - 2 * odd, h)
    down = (block(-2), (h + flip_v) % 2)
    up = (block(2), (h + flip_t) % 2)

    load_t = pltpu.make_async_copy(t_hbm, rows_buf.at[0], load_sem.at[0])
    load_v = pltpu.make_async_copy(v_hbm, rows_buf.at[6], load_sem.at[1])
    load_t.start()
    load_v.start()

    barrier = pltpu.get_barrier_semaphore()
    peers = [other] + [(block(by), q) for by in (-2, -1, 1, 2) for q in (0, 1)]
    for peer in peers:
        pl.semaphore_signal(barrier, inc=1, device_id=peer, device_id_type=MESH)
    pl.semaphore_wait(barrier, len(peers))

    scale = scale_ref[0]
    scale2 = scale * LOG2E

    def copy(slot, k):
        where = slot % 6
        is_v = slot // 6
        if where == 1:
            source, peer = slot - 1, other
        elif where == 4:
            source, peer = slot - 4, (up if is_v else down)
        elif where == 5:
            source, peer = slot - 4, (up if is_v else down)
        else:
            ahead = odd if is_v else 1 - odd
            source, peer = 6 * is_v + (where - 2) + 4 * ahead, mate
        at = pl.ds(pl.multiple_of(k * chunk, chunk), chunk)
        return pltpu.make_async_remote_copy(
            rows_buf.at[source, at], rows_buf.at[slot, at],
            send_sem.at[slot, k], recv_sem.at[slot, k], device_id=peer, device_id_type=MESH,
        )

    def send_all(slot, first=0):
        @pl.loop(first, CHUNKS)
        def _(k):
            copy(slot, k).start()

    def arrived(slot, k):
        at = pl.ds(pl.multiple_of(k * chunk, chunk), chunk)
        pltpu.make_async_remote_copy(
            rows_buf.at[slot, at], rows_buf.at[slot, at],
            send_sem.at[1, 0], recv_sem.at[slot, k], device_id=other, device_id_type=MESH,
        ).wait_recv()

    def part_arrived(slot, part):
        @pl.loop(0, per_part)
        def _(k):
            arrived(slot, part * per_part + k)

    load_t.wait()
    send_all(1)

    @pl.when(odd == 0)
    def _():
        send_all(4)

    load_v.wait()

    @pl.when(odd == 1)
    def _():
        send_all(10)
        send_all(2)

    @pl.when(odd == 0)
    def _():
        send_all(8)

    peak[...] = jnp.full(peak.shape, LOW, jnp.float32)
    total[...] = jnp.zeros(total.shape, jnp.float32)
    acc[...] = jnp.zeros(acc.shape, jnp.float32)

    def first_events(k):
        arrived(1, k)

        @pl.when(odd == 0)
        def _():
            copy(5, k).start()

            @pl.when(k < per_part)
            def _():
                for j in range(2):
                    arrived(4, 2 * k + j)
                    copy(2, 2 * k + j).start()

            @pl.when(k >= per_part)
            def _():
                for j in range(2):
                    arrived(5, 2 * (k - per_part) + j)
                    copy(3, 2 * (k - per_part) + j).start()

            @pl.when(k == per_part)
            def _():
                send_all(10)

        @pl.when(odd == 1)
        def _():
            copy(3, k).start()

            @pl.when(k < per_part)
            def _():
                for j in range(2):
                    arrived(10, 2 * k + j)
                    copy(8, 2 * k + j).start()

        @pl.when(k == CHUNKS - 2)
        def _():
            copy(7, 0).start()

        @pl.when(k == CHUNKS - 1)
        def _():
            send_all(7, 1)

            @pl.when(odd == 1)
            def _():
                send_all(4)
                send_all(5)

    def half_of(part):
        return pl.ds(pl.multiple_of(part * part_rows, part_rows), part_rows)

    def product(left, slot, part):
        return (
            lax.dot_general(
                rows_buf[left], rows_buf[slot, half_of(part)], (((1,), (1,)), ((), ())),
                preferred_element_type=jnp.float32,
            )
            * scale2
        )

    @pl.loop(0, len(FIRST_EVEN))
    def _(n):
        upto, slot, part = looked_up(n, odd, FIRST_EVEN, FIRST_ODD)
        since, _, _ = looked_up(jnp.maximum(n - 1, 0), odd, FIRST_EVEN, FIRST_ODD)

        @pl.loop(since, upto)
        def _(k):
            first_events(k)

        @pl.when((slot == 2) | (slot == 3))
        def _():
            part_arrived(slot, part)

        far = jnp.where((odd == 1) & (slot >= 4), 1, 0)
        tile = product(6 + 4 * far, slot - 4 * far, part)
        scores[slot, :, half_of(part)] = tile
        before = peak[far]
        now = jnp.maximum(before, tile.max(axis=1, keepdims=True))
        peak[far] = now
        summed = jnp.exp2(tile - wide(now, part_rows)).sum(axis=1, keepdims=True)
        total[far] = total[far] * jnp.exp2(before - now) + summed
        top = tile.max(axis=0, keepdims=True)
        own_col[slot, :, half_of(part)] = top + log2(jnp.exp2(tile - top).sum(axis=0, keepdims=True))

        early = jnp.where(odd == 1, n < 6, (n < 2) | ((n >= 7) & (n < 9)))

        @pl.when(early)
        def _():
            even_slot = jnp.where(n < 2, 6, 8)
            even_part = jnp.where(n < 2, n, n - 7)
            e_slot = jnp.where(odd == 1, 6 + 2 * (n // 2), even_slot)
            e_part = jnp.where(odd == 1, n % 2, even_part)

            @pl.when(e_slot == 8)
            def _():
                part_arrived(8, e_part)

            scores[e_slot, :, half_of(e_part)] = product(0, e_slot, e_part)

    label_next = (h + odd * flip_t) % 2
    label_after = (h + flip_t) % 2

    def small(source, target, sends, recvs, at, peer):
        return pltpu.make_async_remote_copy(
            source, target, sends, recvs.at[at], device_id=peer, device_id_type=MESH
        )

    @pl.when(odd == 1)
    def _():
        for slot in range(2):
            own_col[slot] = merged(own_col[slot], own_col[slot + 4])

    col_to = small(own_col.at[1], got_col.at[1], col_send.at[1], col_recv, 1, other)
    col_next = [
        small(own_col.at[2 + j], got_col.at[2 + h], col_send.at[2 + j], col_recv, 2 + h, (block(1), (label_next + j) % 2))
        for j in range(2)
    ]
    col_after = [
        small(own_col.at[4 + j], got_col.at[4 + h], col_send.at[4 + j], col_recv, 4 + h, (block(2), (label_after + j) % 2))
        for j in range(2)
    ]
    row_back = small(own_row.at[1], got_row.at[0], row_send.at[0], row_recv, 0, down)
    for each in [*col_next, col_to]:
        each.start()

    @pl.when(odd == 0)
    def _():
        for each in col_after:
            each.start()

    @pl.when(odd == 1)
    def _():
        own_row[1] = jnp.transpose(peak[1] + log2(total[1]))[:1]
        row_back.start()
        for slot in (4, 5):
            got_col[slot] = jnp.full(got_col.shape[1:], LOW, jnp.float32)

    own_row[0] = jnp.transpose(peak[0] + log2(total[0]))[:1]
    same = lax.broadcasted_iota(jnp.int32, (half, half), 0) == lax.broadcasted_iota(jnp.int32, (half, half), 1)
    diagonal[...] = jnp.where(same, scores[0], 0.0).sum(axis=0, keepdims=True)

    @pl.when(odd == 0)
    def _():
        lanes[6] = own_row[0]

    @pl.when(odd == 1)
    def _():
        row_back.wait_recv()
        lanes[6] = merged(own_row[0], got_row[0])

    row_to = [small(lanes.at[6], lanes.at[7], lane_send.at[6], lane_recv, 7, other)]
    row_to += [
        small(lanes.at[6], lanes.at[6 + 2 * by + h], lane_send.at[5 + 2 * by + q], lane_recv, 6 + 2 * by + h, (block(by), q))
        for by in (1, 2) for q in (0, 1)
    ]
    for each in row_to:
        each.start()

    def col_arrived(at):
        small(own_col.at[1], got_col.at[at], col_send.at[1], col_recv, at, other).wait_recv()

    for at in (1, 2, 3):
        col_arrived(at)

    @pl.when(odd == 0)
    def _():
        for at in (4, 5):
            col_arrived(at)

    terms = [own_col[0]] + [got_col[at] for at in range(1, 6)]
    top = functools.reduce(jnp.maximum, terms)
    lanes[0] = top + log2(functools.reduce(jnp.add, [jnp.exp2(term - top) for term in terms]))
    col_back = [small(lanes.at[0], lanes.at[1], lane_send.at[0], lane_recv, 1, other)]
    col_back += [
        small(lanes.at[0], lanes.at[2 * by + h], lane_send.at[2 * by - 1 + q], lane_recv, 2 * by + h, (block(-by), q))
        for by in (1, 2) for q in (0, 1)
    ]
    for each in col_back:
        each.start()

    def spread(row):
        return jnp.transpose(jnp.broadcast_to(row, (128, half)))

    column[0] = spread(lanes[6])
    column[1] = spread(lanes[0])
    losses[0] = LN2 * (lanes[6] - diagonal[...])
    losses[1] = LN2 * (lanes[0] - diagonal[...])
    loss_out = [
        pltpu.make_async_copy(losses.at[i], ref, out_sem.at[i]) for i, ref in enumerate((image_loss, text_loss))
    ]
    for each in loss_out:
        each.start()

    @pl.loop(1, 6)
    def _(at):
        for base in (0, 6):
            small(lanes.at[0], lanes.at[base + at], lane_send.at[0], lane_recv, base + at, other).wait_recv()

    def second_events(k):
        @pl.when(k < CHUNKS)
        def _():
            arrived(7, k)
            copy(11, k).start()

            @pl.when(odd == 0)
            def _():
                copy(9, k).start()

        @pl.when((k > 0) & (odd == 1))
        def _():
            arrived(11, k - 1)
            copy(9, k - 1).start()

    def lane_of(slot):
        where = slot % 6
        side = slot // 6
        flipped = jnp.where(side == 0, flip_t, flip_v)
        straight = (where < 4) & (odd == side)
        label = (h + jnp.where(straight, 0, flipped) + where % 2) % 2
        return jnp.where(where < 2, slot, slot - where % 2 + label)

    def finish(side, own, ref):
        @pl.loop(0, CHUNKS)
        def _(k):
            at = pl.ds(pl.multiple_of(k * chunk, chunk), chunk)
            acc[side, at] = scale * acc[side, at] - 2.0 * scale * rows_buf[own, at].astype(jnp.float32)

        pltpu.make_async_copy(acc.at[side], ref, out_sem.at[2 + side]).start()

    steps = len(SECOND_EVEN)

    @pl.loop(0, steps)
    def _(n):
        upto, slot, part = looked_up(n, odd, SECOND_EVEN, SECOND_ODD)
        since, _, _ = looked_up(jnp.maximum(n - 1, 0), odd, SECOND_EVEN, SECOND_ODD)
        since = jnp.where(n == 0, 0, since)

        @pl.loop(since, upto)
        def _(k):
            second_events(k)

        side = slot // 6
        late = jnp.where(odd == 1, (slot == 4) | (slot == 5), (slot == 10) | (slot == 11))

        @pl.when(late | (slot == 9))
        def _():
            part_arrived(slot, part)

        @pl.when(late | (slot == 7) | (slot == 9) | (slot == 11))
        def _():
            scores[slot, :, half_of(part)] = product(6 * (1 - side), slot, part)

        tile = scores[slot, :, half_of(part)]
        weights = (
            jnp.exp2(tile - wide(column[side], part_rows)) + jnp.exp2(tile - lanes[lane_of(slot), :, half_of(part)])
        ).astype(jnp.bfloat16)
        for at in range(0, width, 256):
            cols = pl.ds(at, min(256, width))
            acc[side, :, cols] += jnp.dot(
                weights, rows_buf[slot, half_of(part), cols], preferred_element_type=jnp.float32
            )

        @pl.when(n == jnp.where(odd == 1, steps - 1, 11))
        def _():
            finish(0, 0, image_grad)

    finish(1, 6, text_grad)

    @pl.loop(0, CHUNKS)
    def _(k):
        for slot in (1, 2, 3, 4, 5, 7, 8, 9, 10, 11):
            copy(slot, k).wait_send()

    for each in [*col_next, col_to, *row_to, *col_back]:
        each.wait_send()

    @pl.when(odd == 0)
    def _():
        for each in col_after:
            each.wait_send()

    @pl.when(odd == 1)
    def _():
        row_back.wait_send()

    for each in loss_out:
        each.wait()
    for side, ref in enumerate((image_grad, text_grad)):
        pltpu.make_async_copy(acc.at[side], ref, out_sem.at[2 + side]).wait()


def shards(n_dp, group, v, t, scale):
    half, width = v.shape
    f32, bf16 = jnp.float32, jnp.bfloat16
    dma = pltpu.SemaphoreType.DMA
    row = jax.ShapeDtypeStruct((1, half), f32)
    grad = jax.ShapeDtypeStruct((half, width), f32)
    anywhere = pl.BlockSpec(memory_space=pl.ANY)
    image_loss, text_loss, image_grad, text_grad = pl.pallas_call(
        functools.partial(kernel, n_dp, group),
        out_shape=(row, row, grad, grad),
        in_specs=[pl.BlockSpec(memory_space=pltpu.SMEM), anywhere, anywhere],
        out_specs=(anywhere,) * 4,
        scratch_shapes=[
            pltpu.VMEM((12, half, width), bf16),
            pltpu.VMEM((12, half, half), f32),
            pltpu.VMEM((2, half, width), f32),
            pltpu.VMEM((2, half, 128), f32),
            pltpu.VMEM((2, half, 128), f32),
            pltpu.VMEM((6, 1, half), f32),
            pltpu.VMEM((6, 1, half), f32),
            pltpu.VMEM((2, 1, half), f32),
            pltpu.VMEM((1, 1, half), f32),
            pltpu.VMEM((12, 1, half), f32),
            pltpu.VMEM((2, half, 128), f32),
            pltpu.VMEM((2, 1, half), f32),
            pltpu.VMEM((1, half), f32),
            dma((12, CHUNKS)),
            dma((12, CHUNKS)),
            dma((6,)),
            dma((6,)),
            dma((1,)),
            dma((1,)),
            dma((12,)),
            dma((12,)),
            dma((2,)),
            dma((4,)),
        ],
        compiler_params=pltpu.CompilerParams(
            collective_id=0, has_side_effects=True, vmem_limit_bytes=60 << 20
        ),
        cost_estimate=pl.CostEstimate(flops=13_000_000_000, bytes_accessed=6 << 20, transcendentals=10_000_000),
    )(scale, v, t)
    return image_loss.reshape(half), text_loss.reshape(half), image_grad, text_grad


def solution(mesh):
    n_dp = mesh.shape["dp"]
    split = P(("dp", "dup"), None)
    flat = P(("dp", "dup"))
    return jax.shard_map(
        functools.partial(shards, n_dp, n_dp // 2),
        mesh=mesh,
        in_specs=(split, split, P()),
        out_specs=(flat, flat, split, split),
        check_vma=False,
    )
```

time: 390 us -> 110 us (0.28)
  the two profiles are of different devices: /device:TPU:16 before, /device:TPU:1 now
where the time goes in v1:
time: 110 us
  Pallas kernels  101 us (92%)
  local copies, waits for them, and re-layouts  7.14 us (6%)
  between operations  1.29 us (1%)
    pallas_call x1, Pallas kernels, shards(): pl.pallas_call(functools.partial(kernel, n_dp, group), out_shape=(row, ro...  101 us
    unnamed x6, local copies, waits for them, and re-layouts  7.14 us

profile of v1, /device:TPU:1, one launch (start us, length us, event | category | flops | bytes accessed | tf_op | source)
XLA Modules:
  0.0 109.6 jit_solution(11592374839254419051)
XLA Ops:
  1.3 101.2 %shard_map.66 = (f32[1,512]{1,0:T(1,128)}, f32[1,512]{1,0:T(1,128)}, f32[512,1024]{1,0:T(8,128)}, f32[512,1024]{1,0:T(8,128)}) custom-call(f32[1]{0:T(128)S(6)} %copy.11.scale_ref, bf16[512,1024]{1,0:T(8,128)(2,1)} %v_hbm.1, bf16[512,1024]{1,0:T(8,128)(2,1)} %t_hbm.1), custom_call_target="tpu_custom_call" | custom-call | flops 12999999488 | bytes 6291456 | tf_op jit(solution)/shard_map/pallas_call | solution.py:459
  102.5 1.3 %copy.12 = f32[512]{0:T(512)} copy(f32[512]{0:T(512)} %bitcast.3) | data formatting | bytes 4096
  103.7 1.3 %copy.13 = f32[512]{0:T(512)} copy(f32[512]{0:T(512)} %bitcast.2) | data formatting | bytes 4096
  105.0 0.0 copy-start
  105.0 3.3 %copy.14 = f32[512,1024]{1,0:T(8,128)} copy(f32[512,1024]{1,0:T(8,128)} %get-tuple-element.18) | data formatting | bytes 4194304
  108.3 0.0 copy-done
  108.3 1.3 %copy.15 = f32[512,1024]{1,0:T(8,128)} copy(f32[512,1024]{1,0:T(8,128)S(1)} %copy-done) | data formatting | bytes 4194304
Async XLA Ops:
  105.0 3.3 %copy-start = (f32[512,1024]{1,0:T(8,128)S(1)}, f32[512,1024]{1,0:T(8,128)}, u32[]{:S(2)}) copy-start(f32[512,1024]{1,0:T(8,128)} %get-tuple-element.19) | copy-start | bytes 6291460

commit v2 on v1

--- a/solution.py
+++ b/solution.py
@@ -23,16 +23,16 @@
     (6, 5, 0), (7, 2, 1), (7, 3, 0), (8, 1, 1), (8, 5, 1), (8, 3, 1),
 ]
 SECOND_EVEN = [
-    (1, 0, 0), (1, 0, 1), (2, 1, 0), (2, 1, 1), (2, 2, 0), (2, 2, 1),
-    (3, 3, 0), (3, 3, 1), (3, 4, 0), (4, 4, 1), (4, 5, 0), (4, 5, 1),
-    (4, 6, 0), (5, 6, 1), (5, 8, 0), (5, 8, 1), (5, 10, 0), (6, 10, 1),
-    (6, 7, 0), (6, 11, 0), (6, 9, 0), (8, 7, 1), (9, 11, 1), (9, 9, 1),
+    (3, 0, 0), (3, 0, 1), (4, 1, 0), (4, 1, 1), (4, 2, 0), (4, 2, 1),
+    (4, 3, 0), (5, 3, 1), (5, 4, 0), (5, 4, 1), (5, 5, 0), (5, 5, 1),
+    (6, 6, 0), (6, 6, 1), (6, 8, 0), (6, 8, 1), (6, 10, 0), (7, 10, 1),
+    (7, 7, 0), (7, 11, 0), (7, 9, 0), (8, 7, 1), (9, 11, 1), (9, 9, 1),
 ]
 SECOND_ODD = [
-    (1, 0, 0), (1, 0, 1), (2, 1, 0), (2, 1, 1), (2, 2, 0), (2, 2, 1),
-    (3, 3, 0), (3, 3, 1), (3, 6, 0), (4, 6, 1), (4, 8, 0), (4, 8, 1),
-    (4, 10, 0), (5, 10, 1), (5, 4, 0), (5, 4, 1), (5, 5, 0), (6, 7, 0),
-    (6, 11, 0), (6, 9, 0), (8, 7, 1), (9, 11, 1), (9, 9, 1), (9, 5, 1),
+    (3, 0, 0), (3, 0, 1), (4, 1, 0), (4, 1, 1), (4, 2, 0), (4, 2, 1),
+    (4, 3, 0), (5, 3, 1), (5, 6, 0), (5, 6, 1), (5, 8, 0), (5, 8, 1),
+    (6, 10, 0), (6, 10, 1), (6, 4, 0), (6, 4, 1), (6, 7, 0), (7, 11, 0),
+    (7, 9, 0), (7, 5, 0), (8, 7, 1), (9, 5, 1), (9, 11, 1), (9, 9, 1),
 ]
 
 
@@ -67,8 +67,8 @@
     n_dp, group,
     scale_ref, v_hbm, t_hbm,
     image_loss, text_loss, image_grad, text_grad,
-    rows_buf, scores, acc, peak, total, own_col, got_col, own_row, got_row, lanes, column, losses, diagonal,
-    send_sem, recv_sem, col_send, col_recv, row_send, row_recv, lane_send, lane_recv, load_sem, out_sem,
+    rows_buf, scores, acc, peak, total, own_col, got_col, own_row, got_row, lanes, column, diagonal,
+    send_sem, recv_sem, col_send, col_recv, row_send, row_recv, lane_send, lane_recv, load_sem,
 ):
     half, width = v_hbm.shape
     chunk = half // CHUNKS
@@ -121,8 +121,8 @@
             send_sem.at[slot, k], recv_sem.at[slot, k], device_id=peer, device_id_type=MESH,
         )
 
-    def send_all(slot, first=0):
-        @pl.loop(first, CHUNKS)
+    def send_all(slot, first=0, last=CHUNKS):
+        @pl.loop(first, last)
         def _(k):
             copy(slot, k).start()
 
@@ -199,12 +199,11 @@
 
         @pl.when(k == CHUNKS - 1)
         def _():
-            send_all(7, 1)
+            copy(7, 1).start()
 
             @pl.when(odd == 1)
             def _():
-                send_all(4)
-                send_all(5)
+                send_all(4, 0, 2)
 
     def half_of(part):
         return pl.ds(pl.multiple_of(part * part_rows, part_rows), part_rows)
@@ -256,6 +255,21 @@
                 part_arrived(8, e_part)
 
             scores[e_slot, :, half_of(e_part)] = product(0, e_slot, e_part)
+
+    def second_events(k):
+        @pl.when(k < CHUNKS)
+        def _():
+            arrived(7, k)
+            copy(11, k).start()
+
+            @pl.when(odd == 0)
+            def _():
+                copy(9, k).start()
+
+        @pl.when((k > 0) & (odd == 1))
+        def _():
+            arrived(11, k - 1)
+            copy(9, k - 1).start()
 
     label_next = (h + odd * flip_t) % 2
     label_after = (h + flip_t) % 2
@@ -295,6 +309,12 @@
         for slot in (4, 5):
             got_col[slot] = jnp.full(got_col.shape[1:], LOW, jnp.float32)
 
+    send_all(7, 2, 4)
+
+    @pl.when(odd == 1)
+    def _():
+        send_all(4, 2, 6)
+
     own_row[0] = jnp.transpose(peak[0] + log2(total[0]))[:1]
     same = lax.broadcasted_iota(jnp.int32, (half, half), 0) == lax.broadcasted_iota(jnp.int32, (half, half), 1)
     diagonal[...] = jnp.where(same, scores[0], 0.0).sum(axis=0, keepdims=True)
@@ -313,8 +333,7 @@
         small(lanes.at[6], lanes.at[6 + 2 * by + h], lane_send.at[5 + 2 * by + q], lane_recv, 6 + 2 * by + h, (block(by), q))
         for by in (1, 2) for q in (0, 1)
     ]
-    for each in row_to:
-        each.start()
+    second_events(0)
 
     def col_arrived(at):
         small(own_col.at[1], got_col.at[at], col_send.at[1], col_recv, at, other).wait_recv()
@@ -335,41 +354,35 @@
         small(lanes.at[0], lanes.at[2 * by + h], lane_send.at[2 * by - 1 + q], lane_recv, 2 * by + h, (block(-by), q))
         for by in (1, 2) for q in (0, 1)
     ]
-    for each in col_back:
+    for each in [*col_back, *row_to]:
         each.start()
+
+    send_all(7, 4)
+
+    @pl.when(odd == 1)
+    def _():
+        send_all(4, 6)
+        send_all(5)
+
+    second_events(1)
 
     def spread(row):
         return jnp.transpose(jnp.broadcast_to(row, (128, half)))
 
     column[0] = spread(lanes[6])
     column[1] = spread(lanes[0])
-    losses[0] = LN2 * (lanes[6] - diagonal[...])
-    losses[1] = LN2 * (lanes[0] - diagonal[...])
-    loss_out = [
-        pltpu.make_async_copy(losses.at[i], ref, out_sem.at[i]) for i, ref in enumerate((image_loss, text_loss))
-    ]
-    for each in loss_out:
-        each.start()
+    image_loss[...] = LN2 * (lanes[6] - diagonal[...])
+    text_loss[...] = LN2 * (lanes[0] - diagonal[...])
+    @pl.when(odd == 0)
+    def _():
+        for part in range(2):
+            part_arrived(10, part)
+            scores[10, :, half_of(part)] = product(0, 10, part)
 
     @pl.loop(1, 6)
     def _(at):
         for base in (0, 6):
             small(lanes.at[0], lanes.at[base + at], lane_send.at[0], lane_recv, base + at, other).wait_recv()
-
-    def second_events(k):
-        @pl.when(k < CHUNKS)
-        def _():
-            arrived(7, k)
-            copy(11, k).start()
-
-            @pl.when(odd == 0)
-            def _():
-                copy(9, k).start()
-
-        @pl.when((k > 0) & (odd == 1))
-        def _():
-            arrived(11, k - 1)
-            copy(9, k - 1).start()
 
     def lane_of(slot):
         where = slot % 6
@@ -383,9 +396,8 @@
         @pl.loop(0, CHUNKS)
         def _(k):
             at = pl.ds(pl.multiple_of(k * chunk, chunk), chunk)
-            acc[side, at] = scale * acc[side, at] - 2.0 * scale * rows_buf[own, at].astype(jnp.float32)
-
-        pltpu.make_async_copy(acc.at[side], ref, out_sem.at[2 + side]).start()
+            ref[at] = scale * acc[side, at] - 2.0 * scale * rows_buf[own, at].astype(jnp.float32)
+
 
     steps = len(SECOND_EVEN)
 
@@ -393,14 +405,14 @@
     def _(n):
         upto, slot, part = looked_up(n, odd, SECOND_EVEN, SECOND_ODD)
         since, _, _ = looked_up(jnp.maximum(n - 1, 0), odd, SECOND_EVEN, SECOND_ODD)
-        since = jnp.where(n == 0, 0, since)
+        since = jnp.where(n == 0, 2, since)
 
         @pl.loop(since, upto)
         def _(k):
             second_events(k)
 
         side = slot // 6
-        late = jnp.where(odd == 1, (slot == 4) | (slot == 5), (slot == 10) | (slot == 11))
+        late = jnp.where(odd == 1, (slot == 4) | (slot == 5), slot == 11)
 
         @pl.when(late | (slot == 9))
         def _():
@@ -443,10 +455,15 @@
     def _():
         row_back.wait_send()
 
-    for each in loss_out:
+
+def placed(*refs):
+    half = len(refs) // 2
+    sources, targets, sem = refs[:half], refs[half : 2 * half], refs[2 * half]
+    copies = [pltpu.make_async_copy(a, b, sem.at[i]) for i, (a, b) in enumerate(zip(sources, targets))]
+    for each in copies:
+        each.start()
+    for each in copies:
         each.wait()
-    for side, ref in enumerate((image_grad, text_grad)):
-        pltpu.make_async_copy(acc.at[side], ref, out_sem.at[2 + side]).wait()
 
 
 def shards(n_dp, group, v, t, scale):
@@ -455,12 +472,13 @@
     dma = pltpu.SemaphoreType.DMA
     row = jax.ShapeDtypeStruct((1, half), f32)
     grad = jax.ShapeDtypeStruct((half, width), f32)
-    anywhere = pl.BlockSpec(memory_space=pl.ANY)
-    image_loss, text_loss, image_grad, text_grad = pl.pallas_call(
+    near = pl.BlockSpec(memory_space=pltpu.VMEM)
+    far = pl.BlockSpec(memory_space=pltpu.HBM)
+    results = pl.pallas_call(
         functools.partial(kernel, n_dp, group),
         out_shape=(row, row, grad, grad),
-        in_specs=[pl.BlockSpec(memory_space=pltpu.SMEM), anywhere, anywhere],
-        out_specs=(anywhere,) * 4,
+        in_specs=[pl.BlockSpec(memory_space=pltpu.SMEM), far, far],
+        out_specs=(near,) * 4,
         scratch_shapes=[
             pltpu.VMEM((12, half, width), bf16),
             pltpu.VMEM((12, half, half), f32),
@@ -473,7 +491,6 @@
             pltpu.VMEM((1, 1, half), f32),
             pltpu.VMEM((12, 1, half), f32),
             pltpu.VMEM((2, half, 128), f32),
-            pltpu.VMEM((2, 1, half), f32),
             pltpu.VMEM((1, half), f32),
             dma((12, CHUNKS)),
             dma((12, CHUNKS)),
@@ -484,13 +501,20 @@
             dma((12,)),
             dma((12,)),
             dma((2,)),
-            dma((4,)),
         ],
         compiler_params=pltpu.CompilerParams(
-            collective_id=0, has_side_effects=True, vmem_limit_bytes=60 << 20
+            collective_id=0, has_side_effects=True, vmem_limit_bytes=44 << 20
         ),
         cost_estimate=pl.CostEstimate(flops=13_000_000_000, bytes_accessed=6 << 20, transcendentals=10_000_000),
     )(scale, v, t)
+    image_loss, text_loss, image_grad, text_grad = pl.pallas_call(
+        placed,
+        out_shape=(row, row, grad, grad),
+        in_specs=[near] * 4,
+        out_specs=(far,) * 4,
+        scratch_shapes=[dma((4,))],
+        compiler_params=pltpu.CompilerParams(vmem_limit_bytes=8 << 20),
+    )(*results)
     return image_loss.reshape(half), text_loss.reshape(half), image_grad, text_grad
 
 

time: 110 us -> 91.3 us (0.83)
  Pallas kernels: 101 us -> 87.3 us
  local copies, waits for them, and re-layouts: 7.14 us -> 2.44 us
    pallas_call x1, Pallas kernels: 101 us -> 85.3 us  [shards(): pl.pallas_call(functools.partial(kernel, n_dp, group), out_shape=(row, ro...]
    unnamed x6 -> x4, local copies, waits for them, and re-layouts: 7.14 us -> 2.44 us
    pallas_call x0 -> x1, Pallas kernels: none -> 2.05 us  [shards(): pl.pallas_call(placed, out_shape=(row, row, grad, grad), in_specs=[near]...]
where the time goes in v2:
time: 91.3 us; the launch traced here: 91.1 us
  Pallas kernels  87.3 us (96%)
  local copies, waits for them, and re-layouts  2.44 us (3%)
  between operations  1.29 us (1%)
    pallas_call x1, Pallas kernels, shards(): pl.pallas_call(functools.partial(kernel, n_dp, group), out_shape=(row, ro...  85.3 us
    unnamed x4, local copies, waits for them, and re-layouts  2.44 us
    pallas_call x1, Pallas kernels, shards(): pl.pallas_call(placed, out_shape=(row, row, grad, grad), in_specs=[near]...  2.05 us

profile of v2, /device:TPU:1, one launch (start us, length us, event | category | flops | bytes accessed | tf_op | source)
XLA Modules:
  0.0 91.1 jit_solution(555843155975441933)
XLA Ops:
  1.3 0.0 copy-start
  1.3 1.2 %copy-done = bf16[512,1024]{1,0:T(8,128)(2,1)S(1)} copy-done((bf16[512,1024]{1,0:T(8,128)(2,1)S(1)}, bf16[512,1024]{1,0:T(8,128)(2,1)}, u32[]{:S(2)}) %copy-start) | copy-done | bytes 1048600
  2.5 0.0 copy-start.1
  2.5 1.2 %copy-done.1 = bf16[512,1024]{1,0:T(8,128)(2,1)S(1)} copy-done((bf16[512,1024]{1,0:T(8,128)(2,1)S(1)}, bf16[512,1024]{1,0:T(8,128)(2,1)}, u32[]{:S(2)}) %copy-start.1) | copy-done | bytes 1048600
  3.7 85.3 %shard_map.66 = (f32[1,512]{1,0:T(1,128)S(1)}, f32[1,512]{1,0:T(1,128)S(1)}, f32[512,1024]{1,0:T(8,128)S(1)}, f32[512,1024]{1,0:T(8,128)S(1)}) custom-call(f32[1]{0:T(128)S(6)} %copy.7.scale_ref, bf16[512,1024]{1,0:T(8,128)(2,1)S(1)} %copy-done, bf16[512,1024]{1,0:T(8,128)(2,1)S(1)} %copy-done.1), custom_call_target="tpu_custom_call" | custom-call | flops 12999999488 | bytes 6291456 | tf_op jit(solution)/shard_map/pallas_call | solution.py:477
  89.0 2.1 %shard_map.67 = (f32[1,512]{1,0:T(1,128)}, f32[1,512]{1,0:T(1,128)}, f32[512,1024]{1,0:T(8,128)}, f32[512,1024]{1,0:T(8,128)}) custom-call(f32[1,512]{1,0:T(1,128)S(1)} %get-tuple-element.12.refs_0_, f32[1,512]{1,0:T(1,128)S(1)} %get-tuple-element.13.refs_1_, f32[512,1024]{1,0:T(8,128)S(1)} %get-tuple-element.14.refs_2_, ...), custom_call_target="tpu_custom_call" | custom-call | tf_op jit(solution)/shard_map/pallas_call | solution.py:510
Async XLA Ops:
  1.3 1.2 %copy-start = (bf16[512,1024]{1,0:T(8,128)(2,1)S(1)}, bf16[512,1024]{1,0:T(8,128)(2,1)}, u32[]{:S(2)}) copy-start(bf16[512,1024]{1,0:T(8,128)(2,1)} %v_hbm.1) | copy-start | bytes 3145732
  2.5 1.2 %copy-start.1 = (bf16[512,1024]{1,0:T(8,128)(2,1)S(1)}, bf16[512,1024]{1,0:T(8,128)(2,1)}, u32[]{:S(2)}) copy-start(bf16[512,1024]{1,0:T(8,128)(2,1)} %t_hbm.1) | copy-start | bytes 3145732

commit v3 on v2

--- a/solution.py
+++ b/solution.py
@@ -23,16 +23,16 @@
     (6, 5, 0), (7, 2, 1), (7, 3, 0), (8, 1, 1), (8, 5, 1), (8, 3, 1),
 ]
 SECOND_EVEN = [
-    (3, 0, 0), (3, 0, 1), (4, 1, 0), (4, 1, 1), (4, 2, 0), (4, 2, 1),
-    (4, 3, 0), (5, 3, 1), (5, 4, 0), (5, 4, 1), (5, 5, 0), (5, 5, 1),
-    (6, 6, 0), (6, 6, 1), (6, 8, 0), (6, 8, 1), (6, 10, 0), (7, 10, 1),
+    (3, 0, 0), (3, 0, 1), (3, 6, 0), (3, 6, 1), (4, 8, 0), (4, 8, 1),
+    (4, 10, 0), (4, 10, 1), (5, 1, 0), (5, 1, 1), (5, 2, 0), (5, 2, 1),
+    (5, 3, 0), (6, 3, 1), (6, 4, 0), (6, 4, 1), (6, 5, 0), (7, 5, 1),
     (7, 7, 0), (7, 11, 0), (7, 9, 0), (8, 7, 1), (9, 11, 1), (9, 9, 1),
 ]
 SECOND_ODD = [
-    (3, 0, 0), (3, 0, 1), (4, 1, 0), (4, 1, 1), (4, 2, 0), (4, 2, 1),
-    (4, 3, 0), (5, 3, 1), (5, 6, 0), (5, 6, 1), (5, 8, 0), (5, 8, 1),
-    (6, 10, 0), (6, 10, 1), (6, 4, 0), (6, 4, 1), (6, 7, 0), (7, 11, 0),
-    (7, 9, 0), (7, 5, 0), (8, 7, 1), (9, 5, 1), (9, 11, 1), (9, 9, 1),
+    (3, 0, 0), (3, 0, 1), (3, 6, 0), (3, 6, 1), (4, 8, 0), (4, 8, 1),
+    (4, 10, 0), (4, 10, 1), (5, 1, 0), (5, 1, 1), (5, 2, 0), (5, 2, 1),
+    (5, 3, 0), (6, 3, 1), (6, 4, 0), (6, 4, 1), (7, 7, 0), (7, 11, 0),
+    (7, 9, 0), (7, 5, 0), (8, 7, 1), (8, 5, 1), (9, 11, 1), (9, 9, 1),
 ]
 
 
@@ -179,7 +179,7 @@
                     arrived(5, 2 * (k - per_part) + j)
                     copy(3, 2 * (k - per_part) + j).start()
 
-            @pl.when(k == per_part)
+            @pl.when(k == 2)
             def _():
                 send_all(10)
 
@@ -199,8 +199,6 @@
 
         @pl.when(k == CHUNKS - 1)
         def _():
-            copy(7, 1).start()
-
             @pl.when(odd == 1)
             def _():
                 send_all(4, 0, 2)
@@ -309,31 +307,36 @@
         for slot in (4, 5):
             got_col[slot] = jnp.full(got_col.shape[1:], LOW, jnp.float32)
 
-    send_all(7, 2, 4)
-
-    @pl.when(odd == 1)
-    def _():
-        send_all(4, 2, 6)
-
     own_row[0] = jnp.transpose(peak[0] + log2(total[0]))[:1]
     same = lax.broadcasted_iota(jnp.int32, (half, half), 0) == lax.broadcasted_iota(jnp.int32, (half, half), 1)
     diagonal[...] = jnp.where(same, scores[0], 0.0).sum(axis=0, keepdims=True)
-
-    @pl.when(odd == 0)
-    def _():
-        lanes[6] = own_row[0]
-
-    @pl.when(odd == 1)
-    def _():
-        row_back.wait_recv()
-        lanes[6] = merged(own_row[0], got_row[0])
 
     row_to = [small(lanes.at[6], lanes.at[7], lane_send.at[6], lane_recv, 7, other)]
     row_to += [
         small(lanes.at[6], lanes.at[6 + 2 * by + h], lane_send.at[5 + 2 * by + q], lane_recv, 6 + 2 * by + h, (block(by), q))
         for by in (1, 2) for q in (0, 1)
     ]
+
+    @pl.when(odd == 0)
+    def _():
+        lanes[6] = own_row[0]
+        for each in row_to:
+            each.start()
+
+    send_all(7, 1, 3)
+
+    @pl.when(odd == 1)
+    def _():
+        send_all(4, 2, 5)
+
     second_events(0)
+
+    @pl.when(odd == 1)
+    def _():
+        row_back.wait_recv()
+        lanes[6] = merged(own_row[0], got_row[0])
+        for each in row_to:
+            each.start()
 
     def col_arrived(at):
         small(own_col.at[1], got_col.at[at], col_send.at[1], col_recv, at, other).wait_recv()
@@ -354,17 +357,18 @@
         small(lanes.at[0], lanes.at[2 * by + h], lane_send.at[2 * by - 1 + q], lane_recv, 2 * by + h, (block(-by), q))
         for by in (1, 2) for q in (0, 1)
     ]
-    for each in [*col_back, *row_to]:
+    for each in col_back:
         each.start()
 
-    send_all(7, 4)
-
-    @pl.when(odd == 1)
-    def _():
-        send_all(4, 6)
+    send_all(7, 3)
+
+    @pl.when(odd == 1)
+    def _():
+        send_all(4, 5)
         send_all(5)
 
     second_events(1)
+    second_events(2)
 
     def spread(row):
         return jnp.transpose(jnp.broadcast_to(row, (128, half)))
@@ -373,17 +377,6 @@
     column[1] = spread(lanes[0])
     image_loss[...] = LN2 * (lanes[6] - diagonal[...])
     text_loss[...] = LN2 * (lanes[0] - diagonal[...])
-    @pl.when(odd == 0)
-    def _():
-        for part in range(2):
-            part_arrived(10, part)
-            scores[10, :, half_of(part)] = product(0, 10, part)
-
-    @pl.loop(1, 6)
-    def _(at):
-        for base in (0, 6):
-            small(lanes.at[0], lanes.at[base + at], lane_send.at[0], lane_recv, base + at, other).wait_recv()
-
     def lane_of(slot):
         where = slot % 6
         side = slot // 6
@@ -405,14 +398,14 @@
     def _(n):
         upto, slot, part = looked_up(n, odd, SECOND_EVEN, SECOND_ODD)
         since, _, _ = looked_up(jnp.maximum(n - 1, 0), odd, SECOND_EVEN, SECOND_ODD)
-        since = jnp.where(n == 0, 2, since)
+        since = jnp.where(n == 0, 3, since)
 
         @pl.loop(since, upto)
         def _(k):
             second_events(k)
 
         side = slot // 6
-        late = jnp.where(odd == 1, (slot == 4) | (slot == 5), slot == 11)
+        late = jnp.where(odd == 1, (slot == 4) | (slot == 5), (slot == 10) | (slot == 11))
 
         @pl.when(late | (slot == 9))
         def _():
@@ -421,10 +414,16 @@
         @pl.when(late | (slot == 7) | (slot == 9) | (slot == 11))
         def _():
             scores[slot, :, half_of(part)] = product(6 * (1 - side), slot, part)
+
+        lane = lane_of(slot)
+
+        @pl.when((part == 0) & (slot % 6 > 0))
+        def _():
+            small(lanes.at[0], lanes.at[lane], lane_send.at[0], lane_recv, lane, other).wait_recv()
 
         tile = scores[slot, :, half_of(part)]
         weights = (
-            jnp.exp2(tile - wide(column[side], part_rows)) + jnp.exp2(tile - lanes[lane_of(slot), :, half_of(part)])
+            jnp.exp2(tile - wide(column[side], part_rows)) + jnp.exp2(tile - lanes[lane, :, half_of(part)])
         ).astype(jnp.bfloat16)
         for at in range(0, width, 256):
             cols = pl.ds(at, min(256, width))
@@ -432,7 +431,7 @@
                 weights, rows_buf[slot, half_of(part), cols], preferred_element_type=jnp.float32
             )
 
-        @pl.when(n == jnp.where(odd == 1, steps - 1, 11))
+        @pl.when(n == jnp.where(odd == 1, 21, 17))
         def _():
             finish(0, 0, image_grad)
 

time: 91.3 us -> 86.2 us (0.944)
  Pallas kernels: 87.3 us -> 82.3 us
    pallas_call x1, Pallas kernels: 85.3 us -> 80.3 us  [shards(): pl.pallas_call(functools.partial(kernel, n_dp, group), out_shape=(row, ro...]
where the time goes in v3:
time: 86.2 us; the launch traced here: 86 us
  Pallas kernels  82.3 us (95%)
  local copies, waits for them, and re-layouts  2.44 us (3%)
  between operations  1.29 us (1%)
    pallas_call x1, Pallas kernels, shards(): pl.pallas_call(functools.partial(kernel, n_dp, group), out_shape=(row, ro...  80.3 us
    unnamed x4, local copies, waits for them, and re-layouts  2.44 us
    pallas_call x1, Pallas kernels, shards(): pl.pallas_call(placed, out_shape=(row, row, grad, grad), in_specs=[near]...  2.05 us

profile of v3, /device:TPU:1, one launch (start us, length us, event | category | flops | bytes accessed | tf_op | source)
XLA Modules:
  0.0 86.0 jit_solution(15834151240078585055)
XLA Ops:
  1.3 0.0 copy-start
  1.3 1.2 %copy-done = bf16[512,1024]{1,0:T(8,128)(2,1)S(1)} copy-done((bf16[512,1024]{1,0:T(8,128)(2,1)S(1)}, bf16[512,1024]{1,0:T(8,128)(2,1)}, u32[]{:S(2)}) %copy-start) | copy-done | bytes 1048600
  2.5 0.0 copy-start.1
  2.5 1.2 %copy-done.1 = bf16[512,1024]{1,0:T(8,128)(2,1)S(1)} copy-done((bf16[512,1024]{1,0:T(8,128)(2,1)S(1)}, bf16[512,1024]{1,0:T(8,128)(2,1)}, u32[]{:S(2)}) %copy-start.1) | copy-done | bytes 1048600
  3.7 80.3 %shard_map.66 = (f32[1,512]{1,0:T(1,128)S(1)}, f32[1,512]{1,0:T(1,128)S(1)}, f32[512,1024]{1,0:T(8,128)S(1)}, f32[512,1024]{1,0:T(8,128)S(1)}) custom-call(f32[1]{0:T(128)S(6)} %copy.7.scale_ref, bf16[512,1024]{1,0:T(8,128)(2,1)S(1)} %copy-done, bf16[512,1024]{1,0:T(8,128)(2,1)S(1)} %copy-done.1), custom_call_target="tpu_custom_call" | custom-call | flops 12999999488 | bytes 6291456 | tf_op jit(solution)/shard_map/pallas_call | solution.py:476
  84.0 2.1 %shard_map.67 = (f32[1,512]{1,0:T(1,128)}, f32[1,512]{1,0:T(1,128)}, f32[512,1024]{1,0:T(8,128)}, f32[512,1024]{1,0:T(8,128)}) custom-call(f32[1,512]{1,0:T(1,128)S(1)} %get-tuple-element.12.refs_0_, f32[1,512]{1,0:T(1,128)S(1)} %get-tuple-element.13.refs_1_, f32[512,1024]{1,0:T(8,128)S(1)} %get-tuple-element.14.refs_2_, ...), custom_call_target="tpu_custom_call" | custom-call | tf_op jit(solution)/shard_map/pallas_call | solution.py:509
Async XLA Ops:
  1.3 1.2 %copy-start = (bf16[512,1024]{1,0:T(8,128)(2,1)S(1)}, bf16[512,1024]{1,0:T(8,128)(2,1)}, u32[]{:S(2)}) copy-start(bf16[512,1024]{1,0:T(8,128)(2,1)} %v_hbm.1) | copy-start | bytes 3145732
  2.5 1.2 %copy-start.1 = (bf16[512,1024]{1,0:T(8,128)(2,1)S(1)}, bf16[512,1024]{1,0:T(8,128)(2,1)}, u32[]{:S(2)}) copy-start(bf16[512,1024]{1,0:T(8,128)(2,1)} %t_hbm.1) | copy-start | bytes 3145732

commit v4 on v3

--- a/solution.py
+++ b/solution.py
@@ -23,13 +23,13 @@
     (6, 5, 0), (7, 2, 1), (7, 3, 0), (8, 1, 1), (8, 5, 1), (8, 3, 1),
 ]
 SECOND_EVEN = [
-    (3, 0, 0), (3, 0, 1), (3, 6, 0), (3, 6, 1), (4, 8, 0), (4, 8, 1),
+    (2, 0, 0), (2, 0, 1), (3, 6, 0), (3, 6, 1), (4, 8, 0), (4, 8, 1),
     (4, 10, 0), (4, 10, 1), (5, 1, 0), (5, 1, 1), (5, 2, 0), (5, 2, 1),
     (5, 3, 0), (6, 3, 1), (6, 4, 0), (6, 4, 1), (6, 5, 0), (7, 5, 1),
     (7, 7, 0), (7, 11, 0), (7, 9, 0), (8, 7, 1), (9, 11, 1), (9, 9, 1),
 ]
 SECOND_ODD = [
-    (3, 0, 0), (3, 0, 1), (3, 6, 0), (3, 6, 1), (4, 8, 0), (4, 8, 1),
+    (2, 0, 0), (2, 0, 1), (3, 6, 0), (3, 6, 1), (4, 8, 0), (4, 8, 1),
     (4, 10, 0), (4, 10, 1), (5, 1, 0), (5, 1, 1), (5, 2, 0), (5, 2, 1),
     (5, 3, 0), (6, 3, 1), (6, 4, 0), (6, 4, 1), (7, 7, 0), (7, 11, 0),
     (7, 9, 0), (7, 5, 0), (8, 7, 1), (8, 5, 1), (9, 11, 1), (9, 9, 1),
@@ -116,8 +116,9 @@
             ahead = odd if is_v else 1 - odd
             source, peer = 6 * is_v + (where - 2) + 4 * ahead, mate
         at = pl.ds(pl.multiple_of(k * chunk, chunk), chunk)
+        held = (v_hbm if is_v else t_hbm).at[at] if where in (1, 4) else rows_buf.at[source, at]
         return pltpu.make_async_remote_copy(
-            rows_buf.at[source, at], rows_buf.at[slot, at],
+            held, rows_buf.at[slot, at],
             send_sem.at[slot, k], recv_sem.at[slot, k], device_id=peer, device_id_type=MESH,
         )
 
@@ -138,13 +139,13 @@
         def _(k):
             arrived(slot, part * per_part + k)
 
+    send_all(1)
+
+    @pl.when(odd == 0)
+    def _():
+        send_all(4)
+
     load_t.wait()
-    send_all(1)
-
-    @pl.when(odd == 0)
-    def _():
-        send_all(4)
-
     load_v.wait()
 
     @pl.when(odd == 1)
@@ -308,8 +309,6 @@
             got_col[slot] = jnp.full(got_col.shape[1:], LOW, jnp.float32)
 
     own_row[0] = jnp.transpose(peak[0] + log2(total[0]))[:1]
-    same = lax.broadcasted_iota(jnp.int32, (half, half), 0) == lax.broadcasted_iota(jnp.int32, (half, half), 1)
-    diagonal[...] = jnp.where(same, scores[0], 0.0).sum(axis=0, keepdims=True)
 
     row_to = [small(lanes.at[6], lanes.at[7], lane_send.at[6], lane_recv, 7, other)]
     row_to += [
@@ -330,13 +329,6 @@
         send_all(4, 2, 5)
 
     second_events(0)
-
-    @pl.when(odd == 1)
-    def _():
-        row_back.wait_recv()
-        lanes[6] = merged(own_row[0], got_row[0])
-        for each in row_to:
-            each.start()
 
     def col_arrived(at):
         small(own_col.at[1], got_col.at[at], col_send.at[1], col_recv, at, other).wait_recv()
@@ -360,6 +352,13 @@
     for each in col_back:
         each.start()
 
+    @pl.when(odd == 1)
+    def _():
+        row_back.wait_recv()
+        lanes[6] = merged(own_row[0], got_row[0])
+        for each in row_to:
+            each.start()
+
     send_all(7, 3)
 
     @pl.when(odd == 1)
@@ -368,7 +367,9 @@
         send_all(5)
 
     second_events(1)
-    second_events(2)
+
+    same = lax.broadcasted_iota(jnp.int32, (half, half), 0) == lax.broadcasted_iota(jnp.int32, (half, half), 1)
+    diagonal[...] = jnp.where(same, scores[0], 0.0).sum(axis=0, keepdims=True)
 
     def spread(row):
         return jnp.transpose(jnp.broadcast_to(row, (128, half)))
@@ -398,7 +399,7 @@
     def _(n):
         upto, slot, part = looked_up(n, odd, SECOND_EVEN, SECOND_ODD)
         since, _, _ = looked_up(jnp.maximum(n - 1, 0), odd, SECOND_EVEN, SECOND_ODD)
-        since = jnp.where(n == 0, 3, since)
+        since = jnp.where(n == 0, 2, since)
 
         @pl.loop(since, upto)
         def _(k):

time: 86.2 us -> 86.2 us (level)
  no operation moved by 1% of the time
where the time goes in v4:
time: 86.2 us; the launch traced here: 86 us
  Pallas kernels  82.3 us (95%)
  local copies, waits for them, and re-layouts  2.44 us (3%)
  between operations  1.29 us (1%)
    pallas_call x1, Pallas kernels, shards(): pl.pallas_call(functools.partial(kernel, n_dp, group), out_shape=(row, ro...  80.2 us
    unnamed x4, local copies, waits for them, and re-layouts  2.44 us
    pallas_call x1, Pallas kernels, shards(): pl.pallas_call(placed, out_shape=(row, row, grad, grad), in_specs=[near]...  2.05 us

profile of v4, /device:TPU:1, one launch (start us, length us, event | category | flops | bytes accessed | tf_op | source)
XLA Modules:
  0.0 86.0 jit_solution(10361897617653458442)
XLA Ops:
  1.3 0.0 copy-start
  1.3 1.2 %copy-done = bf16[512,1024]{1,0:T(8,128)(2,1)S(1)} copy-done((bf16[512,1024]{1,0:T(8,128)(2,1)S(1)}, bf16[512,1024]{1,0:T(8,128)(2,1)}, u32[]{:S(2)}) %copy-start) | copy-done | bytes 1048600
  2.5 0.0 copy-start.1
  2.5 1.2 %copy-done.1 = bf16[512,1024]{1,0:T(8,128)(2,1)S(1)} copy-done((bf16[512,1024]{1,0:T(8,128)(2,1)S(1)}, bf16[512,1024]{1,0:T(8,128)(2,1)}, u32[]{:S(2)}) %copy-start.1) | copy-done | bytes 1048600
  3.7 80.2 %shard_map.66 = (f32[1,512]{1,0:T(1,128)S(1)}, f32[1,512]{1,0:T(1,128)S(1)}, f32[512,1024]{1,0:T(8,128)S(1)}, f32[512,1024]{1,0:T(8,128)S(1)}) custom-call(f32[1]{0:T(128)S(6)} %copy.7.scale_ref, bf16[512,1024]{1,0:T(8,128)(2,1)S(1)} %copy-done, bf16[512,1024]{1,0:T(8,128)(2,1)S(1)} %copy-done.1), custom_call_target="tpu_custom_call" | custom-call | flops 12999999488 | bytes 6291456 | tf_op jit(solution)/shard_map/pallas_call | solution.py:477
  83.9 2.1 %shard_map.67 = (f32[1,512]{1,0:T(1,128)}, f32[1,512]{1,0:T(1,128)}, f32[512,1024]{1,0:T(8,128)}, f32[512,1024]{1,0:T(8,128)}) custom-call(f32[1,512]{1,0:T(1,128)S(1)} %get-tuple-element.12.refs_0_, f32[1,512]{1,0:T(1,128)S(1)} %get-tuple-element.13.refs_1_, f32[512,1024]{1,0:T(8,128)S(1)} %get-tuple-element.14.refs_2_, ...), custom_call_target="tpu_custom_call" | custom-call | tf_op jit(solution)/shard_map/pallas_call | solution.py:510
Async XLA Ops:
  1.3 1.2 %copy-start = (bf16[512,1024]{1,0:T(8,128)(2,1)S(1)}, bf16[512,1024]{1,0:T(8,128)(2,1)}, u32[]{:S(2)}) copy-start(bf16[512,1024]{1,0:T(8,128)(2,1)} %v_hbm.1) | copy-start | bytes 3145732
  2.5 1.2 %copy-start.1 = (bf16[512,1024]{1,0:T(8,128)(2,1)S(1)}, bf16[512,1024]{1,0:T(8,128)(2,1)}, u32[]{:S(2)}) copy-start(bf16[512,1024]{1,0:T(8,128)(2,1)} %t_hbm.1) | copy-start | bytes 3145732
